TPU v7x, 256 devices: a whole 4x4x8 slice. The times are simulated.
256 devices in a mesh: row: 32 (over z, x_hi, core), col: 8 (over x_lo, y).
Axes of the slice: x: 4 (x_hi: 2, x_lo: 2; x = x_hi * 2 + x_lo), y: 4, z: 8, core: 2. Of those that a mesh axis runs over, the one named last changes fastest.
Arguments:
- tokens: bfloat16 [512, 256, 512], P('row', 'col'), may hold values from -24 to 24, as said below
- die_mask: int32 [512, 256], P('row', 'col'), may hold values 0 or 1
- expert_ids: int32 [32, 8, 512, 2], P('row', 'col'), may hold values from 0 to 31, all different within a row; in each aligned block of 512 rows (0 to 511, 512 to 1023, ..., all dimensions but the last counted through in order) at most 96 rows name the same one
- gain_attn: float32 [512], replicated, may hold values from 0.25 to 1.75
- w_qkv: bfloat16 [512, 1536], replicated, may hold values from -1 to 1
- w_out: bfloat16 [512, 512], replicated, may hold values from -0.25 to 0.25
- gain_moe: float32 [512], replicated, may hold values from 0.25 to 1.75
- w_router: bfloat16 [512, 32], replicated, may hold values from -0.1875 to 0.1875
- w_in: bfloat16 [32, 512, 2048], P('row'), may hold values from -0.25 to 0.25
- w_down: bfloat16 [32, 2048, 512], P('row'), may hold values from -0.25 to 0.25
Outputs:
- layer_out: bfloat16 [512, 256, 512], P('row', 'col')
Inputs may be any that keep to these rules, and one draw needn't show every extreme that they name: `tokens`: drawn features; at most 24 in magnitude. `expert_ids`: the two ids of a patch differ. Among the 512 patches of one device, no expert is named by more than 96 patches, a bound that some block reaches.
All inputs are finite; a program needn't handle non-finite values. No bound on the sum of `die_mask` on one device may be relied on, other than what follows from the above.
Results may differ from a plain program's by a relative error of at most 0.01.
Values may be sent and summed in bfloat16 or wider, within the bound.
No kernel may reach another device: no remote copies, remote signals or barrier semaphores. Data moves between devices by JAX's collectives and lax.ppermute only.
A program may use at most 128 MiB of HBM per device.

v0:
```python
import jax
import jax.numpy as jnp
from jax import lax
from jax.sharding import PartitionSpec as P

HEADS = 16
RADIUS = 6
CAP = 96


def with_halo(cells, sides, width):
    for axis, dim in sides:
        count = lax.axis_size(axis)
        ends = count - 1
        head = lax.slice_in_dim(cells, 0, width, axis=dim)
        tail = lax.slice_in_dim(cells, cells.shape[dim] - width, cells.shape[dim], axis=dim)
        cells = jnp.concatenate(
            [
                lax.ppermute(tail, axis, [(i, (i + 1) % count) for i in range(ends)]),
                cells,
                lax.ppermute(head, axis, [((i + 1) % count, i) for i in range(ends)]),
            ],
            axis=dim,
        )
    return cells


def rms_norm(values, gain):
    wide = values.astype(jnp.float32)
    power = jnp.mean(wide * wide, axis=-1, keepdims=True)
    return (wide * lax.rsqrt(power + 1e-06) * gain).astype(jnp.bfloat16)


def neighbourhood(query, padded, mask_pad, radius):
    ht, wt, heads, hdim = query.shape
    width = heads * hdim
    block_rows = min(ht, 16)
    block_cols = min(wt, 16)
    key_rows = block_rows + 2 * radius
    key_cols = block_cols + 2 * radius
    across = wt // block_cols
    blocks = ht // block_rows * across
    spots = jnp.arange(block_rows * block_cols, dtype=jnp.int32)
    places = jnp.arange(key_rows * key_cols, dtype=jnp.int32)
    rise = places[None, :] // key_cols - spots[:, None] // block_cols
    reach = places[None, :] % key_cols - spots[:, None] % block_cols
    inside = (rise >= 0) & (rise <= 2 * radius) & (reach >= 0) & (reach <= 2 * radius)
    centre = (rise == radius) & (reach == radius)

    def one_block(index):
        first_row = index // across * block_rows
        first_col = index % across * block_cols
        anchor = jnp.zeros((), jnp.int32)
        queries = lax.dynamic_slice(
            query, (first_row, first_col, anchor, anchor), (block_rows, block_cols, heads, hdim)
        ).reshape(block_rows * block_cols, heads, hdim)
        window = lax.dynamic_slice(
            padded, (first_row, first_col, anchor), (key_rows, key_cols, 2 * width)
        ).reshape(key_rows * key_cols, 2 * width)
        marks = lax.dynamic_slice(mask_pad, (first_row, first_col), (key_rows, key_cols)).reshape(
            key_rows * key_cols
        )
        keys = window[:, :width].reshape(key_rows * key_cols, heads, hdim)
        values = window[:, width:].reshape(key_rows * key_cols, heads, hdim)
        scores = jnp.einsum("qnc,knc->nqk", queries, keys, preferred_element_type=jnp.float32)
        valid = inside & (marks[None, :] > 0.5) | centre
        masked = jnp.where(valid[None], scores, -1e30)
        highest = jnp.max(masked, axis=-1, keepdims=True)
        weights = jnp.exp(masked - highest)
        total = jnp.sum(weights, axis=-1)
        summed = jnp.einsum(
            "nqk,knc->qnc", weights.astype(jnp.bfloat16), values, preferred_element_type=jnp.float32
        )
        return (summed / jnp.transpose(total)[..., None]).astype(jnp.bfloat16)

    done = lax.map(one_block, jnp.arange(blocks, dtype=jnp.int32))
    return (
        done.reshape(ht // block_rows, across, block_rows, block_cols, width)
        .transpose(0, 2, 1, 3, 4)
        .reshape(ht * wt, width)
    )


def per_device(
    tokens, die_mask, expert_ids, gain_attn, w_qkv, w_out, gain_moe, w_router, w_in, w_down
):
    ht, wt, width = tokens.shape
    patches = ht * wt
    heads = HEADS
    hdim = width // heads
    radius = RADIUS
    normed = rms_norm(tokens, gain_attn)
    flat = normed.reshape(patches, width)
    mask_vals = die_mask.astype(jnp.bfloat16)
    proj = jnp.dot(flat, w_qkv, preferred_element_type=jnp.float32)
    query = proj[:, :width]
    pair = proj[:, width:].astype(jnp.bfloat16).reshape(ht, wt, 2 * width)
    padded, mask_pad = (
        with_halo(pair, (("row", 0), ("col", 1)), radius),
        with_halo(mask_vals, (("row", 0), ("col", 1)), radius),
    )
    query = (query * hdim ** (-0.5)).astype(jnp.bfloat16).reshape(ht, wt, heads, hdim)
    attended = neighbourhood(query, padded, mask_pad, radius)
    mixed = jnp.dot(attended, w_out, preferred_element_type=jnp.float32)
    resid = (tokens.reshape(patches, width).astype(jnp.float32) + mixed).astype(jnp.bfloat16)
    normed_moe = rms_norm(resid, gain_moe)
    experts = w_router.shape[1]
    capacity = CAP
    logits = jnp.dot(normed_moe, w_router, preferred_element_type=jnp.float32)
    ids = expert_ids.reshape(patches, 2)
    picks = ids[:, :, None] == jnp.arange(experts, dtype=jnp.int32)[None, None, :]
    chosen = jnp.sum(jnp.where(picks, logits[:, None, :], 0.0), axis=-1)
    gates = jnp.stack(
        [jax.nn.sigmoid(chosen[:, 0] - chosen[:, 1]), jax.nn.sigmoid(chosen[:, 1] - chosen[:, 0])],
        axis=1,
    )
    onehot = picks.reshape(2 * patches, experts).astype(jnp.int32)
    slots = jnp.sum((jnp.cumsum(onehot, axis=0) - 1) * onehot, axis=-1).reshape(patches, 2)
    position = ids * capacity + slots
    lines = jnp.arange(experts * capacity, dtype=jnp.int32)[:, None]
    dispatch = ((lines == position[:, 0][None, :]) | (lines == position[:, 1][None, :])).astype(
        jnp.bfloat16
    )
    outgoing = (
        jnp.dot(dispatch, normed_moe, preferred_element_type=jnp.float32)
        .astype(jnp.bfloat16)
        .reshape(experts, capacity, width)
    )
    sources = lax.axis_size("row")
    held = w_in.shape[0]
    block = lax.all_to_all(outgoing, "row", split_axis=0, concat_axis=0, tiled=True)
    grouped = block.reshape(sources, held, block.shape[1], width)
    hidden = jnp.einsum("secd,edf->secf", grouped, w_in, preferred_element_type=jnp.float32)
    hidden = jax.nn.gelu(hidden, approximate=True).astype(jnp.bfloat16)
    result = jnp.einsum(
        "secf,efd->secd", hidden, w_down, preferred_element_type=jnp.float32
    ).astype(jnp.bfloat16)
    done = result.reshape(sources * held, block.shape[1], width)
    back = lax.all_to_all(done, "row", split_axis=0, concat_axis=0, tiled=True)
    picked = back.reshape(experts * capacity, width)[position.reshape(-1)].reshape(
        patches, 2, width
    )
    moe = jnp.sum(picked.astype(jnp.float32) * gates[..., None], axis=1)
    final = (resid.astype(jnp.float32) + moe).astype(jnp.bfloat16)
    return final.reshape(ht, wt, width)


def solution(mesh):
    return jax.shard_map(
        per_device,
        mesh=mesh,
        in_specs=(
            P("row", "col", None),
            P("row", "col"),
            P("row", "col", None, None),
            P(),
            P(),
            P(),
            P(),
            P(),
            P("row", None, None),
            P("row", None, None),
        ),
        out_specs=P("row", "col", None),
        check_vma=False,
    )
```

profile of v0, /device:TPU:3, one launch (start us, length us, event | category | flops | bytes accessed | tf_op | source)
XLA Modules:
  0.0 344.8 jit_solution(10332631641090468193)
XLA Ops:
  0.0 1.4 multiply_reduce_fusion.1
  2.6 4.0 %fusion.89 = (bf16[512,1536]{1,0:T(8,128)(2,1)S(1)}, f32[512,1536]{1,0:T(8,128)}) fusion(bf16[512,512]{1,0:T(8,128)(2,1)S(1)} %bitcast.113, bf16[512,1536]{1,0:T(8,128)(2,1)} %param.16), kind=kOutput, calls=%fused_computation.121 | convolution fusion | flops 806092800 | bytes 6815744 | tf_op jit(solution)/shard_map/dot_general | solution.py:95
  8.8 4.3 %collective-permute-start = (bf16[6,32,1024]{2,1,0:T(8,128)(2,1)}, bf16[6,32,1024]{2,1,0:T(8,128)(2,1)S(1)}, u32[]{:S(2)}, u32[]{:S(2)}) collective-permute-start(bf16[6,32,1024]{2,1,0:T(8,128)(2,1)} %bitcast.2), channel_id=1, source_target_pairs={{0,8},{8,16},{16,24},{24,32},{32,40},{40,48},{48,56},{56,64},{64,7... | collective-permute-start | bytes 1179656 | tf_op jit(solution)/shard_map/ppermute | solution.py:19
  13.1 1.9 collective-permute-start.1
  15.7 5.1 %collective-permute-start.4 = (bf16[6,32]{1,0:T(8,128)(2,1)}, bf16[6,32]{1,0:T(8,128)(2,1)S(1)}, u32[]{:S(2)}, u32[]{:S(2)}) collective-permute-start(bf16[6,32]{1,0:T(8,128)(2,1)} %get-tuple-element.222), channel_id=1, source_target_pairs={{0,8},{8,16},{16,24},{24,32},{32,40},{40,48},{48,56},{56,64},{64,7... | collective-permute-start | bytes 1160 | tf_op jit(solution)/shard_map/ppermute | solution.py:19
  20.8 1.9 collective-permute-start.5
  23.3 2.1 fusion.65
  25.4 9.0 %reduce-window.6 = s32[32,8,128]{2,1,0:T(8,128)S(1)} reduce-window(s32[32,8,128]{2,1,0:T(8,128)S(1)} %fusion.71, s32[]{:T(128)} %constant.150.clone.1), window={size=1x1x128 pad=0_0x0_0x127_0}, to_apply=%region_5.6 | reduce-window | flops 4161536 | bytes 262148 | tf_op jit(solution)/shard_map/reduce-window
  36.1 1.3 slice.98
  38.7 2.1 pad_maximum_fusion.3
  40.8 3.2 collective-permute-start.2
  44.0 4.2 %collective-permute-start.3 = (bf16[28,6,1024]{2,1,0:T(8,128)(2,1)}, bf16[28,6,1024]{2,1,0:T(8,128)(2,1)}, u32[]{:S(2)}, u32[]{:S(2)}) collective-permute-start(bf16[28,6,1024]{2,1,0:T(8,128)(2,1)} %get-tuple-element.215), channel_id=1, source_target_pairs={{1,0},{2,1},{3,2},{4,3},{5,4},{6,5},{7,6},{9,8},{10,9},{11,10},{12... | collective-permute-start | bytes 1032200 | tf_op jit(solution)/shard_map/ppermute | solution.py:21
  48.9 1.9 collective-permute-start.6
  50.9 5.7 %collective-permute-start.7 = (bf16[28,6]{1,0:T(8,128)(2,1)}, bf16[28,6]{1,0:T(8,128)(2,1)}, u32[]{:S(2)}, u32[]{:S(2)}) collective-permute-start(bf16[28,6]{1,0:T(8,128)(2,1)} %get-tuple-element.219), channel_id=1, source_target_pairs={{1,0},{2,1},{3,2},{4,3},{5,4},{6,5},{7,6},{9,8},{10,9},{11,10},{12... | collective-permute-start | bytes 1016 | tf_op jit(solution)/shard_map/ppermute | solution.py:21
  57.1 3.6 %reshape.277 = bf16[16,32,16,32]{3,2,1,0:T(8,128)(2,1)} reshape(bf16[512,512]{1,0:T(8,128)(2,1)} %fusion.65) | data formatting | bytes 1048576 | tf_op jit(solution)/shard_map/reshape | solution.py:102
  62.1 3.9 %pad_maximum_fusion = bf16[28,44,1024]{2,1,0:T(8,128)(2,1)} fusion(bf16[28,6,1024]{2,1,0:T(8,128)(2,1)} %collective-permute-done.3, bf16[6,32,1024]{2,1,0:T(8,128)(2,1)} %collective-permute-done.1, bf16[16,32,1024]{2,1,0:T(8,128)(2,1)S(1)} %bitcast.111, bf16[6,32,1024]{2,1,0:T(8,128)(2,1)S(1)} %collective-permute-done, ...), kind=kLoop, calls=%fused_computation.51 | loop fusion | flops 12615680 | bytes 5046272 | tf_op jit(solution)/shard_map/concatenate | solution.py:17
  66.0 66.8 %while.14 = (s32[]{:T(128)}, bf16[2,256,16,32]{1,3,2,0:T(8,128)(2,1)}, s32[2]{0:T(128)S(1)}, bf16[28,44,1024]{2,1,0:T(8,128)(2,1)}, bf16[28,44]{1,0:T(8,128)(2,1...) while((s32[]{:T(128)}, ...), condition=%wide.region_4.5_spmd.clone.clone, body=%wide.region_1.4_spmd.clone.clone.sunk | while | flops 439798080 | bytes 109647536 | solution.py:76
  68.5 3.9 %constant_dynamic-slice_fusion.4 = bf16[28,28,1024]{2,1,0:T(8,128)(2,1)} fusion(bf16[28,44,1024]{2,1,0:T(8,128)(2,1)} %get-tuple-element.336, s32[]{:T(128)S(6)} %select_n.148), kind=kLoop, calls=%fused_computation.30.clone.1 | loop fusion | bytes 3211268 | tf_op jit(solution)/shard_map/while/body/eval_jaxpr/dynamic_slice | solution.py:57
  72.4 3.5 %reshape.312 = bf16[784,1024]{1,0:T(8,128)(2,1)} reshape(bf16[28,28,1024]{2,1,0:T(8,128)(2,1)} %constant_dynamic-slice_fusion.4) | data formatting | bytes 3211264 | tf_op jit(solution)/shard_map/while/body/eval_jaxpr/reshape | solution.py:59
  75.9 2.4 fusion.108
  78.4 1.3 copy.78
  79.6 1.4 constant_dynamic-slice_fusion.5
  82.1 3.2 select_reduce_fusion.3
  85.4 2.2 fusion.110
  87.5 2.4 copy-done.1
  89.9 1.3 copy.77
  91.2 8.2 %fusion.111 = bf16[2,256,16,32]{1,3,2,0:T(8,128)(2,1)} fusion(bf16[2,256,16,32]{1,3,2,0:T(8,128)(2,1)} %get-tuple-element.318, s32[]{:T(128)} %get-tuple-element.317, bf16[784,16,32]{0,2,1:T(8,128)(2,1)} %bitcast.109, f32[16,256,784]{1,2,0:T(8,128)} %copy-done.1, f32[16,256]{1,0:T(8,128)S(1)} %get-tuple-element.300, ...), kind=kOutput, calls=%fused_computation.21.clone.1 | convolution fusion | flops 215416832 | bytes 14258688 | tf_op jit(solution)/shard_map/while/body/eval_jaxpr/nqk,knc->qnc/dot_general | solution.py:71
  102.0 3.8 %constant_dynamic-slice_fusion.4 = bf16[28,28,1024]{2,1,0:T(8,128)(2,1)} fusion(bf16[28,44,1024]{2,1,0:T(8,128)(2,1)} %get-tuple-element.336, s32[]{:T(128)S(6)} %select_n.148), kind=kLoop, calls=%fused_computation.30.clone.1 | loop fusion | bytes 3211268 | tf_op jit(solution)/shard_map/while/body/eval_jaxpr/dynamic_slice | solution.py:57
  105.8 3.5 %reshape.312 = bf16[784,1024]{1,0:T(8,128)(2,1)} reshape(bf16[28,28,1024]{2,1,0:T(8,128)(2,1)} %constant_dynamic-slice_fusion.4) | data formatting | bytes 3211264 | tf_op jit(solution)/shard_map/while/body/eval_jaxpr/reshape | solution.py:59
  109.3 2.4 fusion.108
  111.7 1.3 copy.78
  113.0 1.4 constant_dynamic-slice_fusion.5
  115.4 3.2 select_reduce_fusion.3
  118.7 2.2 fusion.110
  120.9 2.4 copy-done.1
  123.3 1.3 copy.77
  124.6 8.2 %fusion.111 = bf16[2,256,16,32]{1,3,2,0:T(8,128)(2,1)} fusion(bf16[2,256,16,32]{1,3,2,0:T(8,128)(2,1)} %get-tuple-element.318, s32[]{:T(128)} %get-tuple-element.317, bf16[784,16,32]{0,2,1:T(8,128)(2,1)} %bitcast.109, f32[16,256,784]{1,2,0:T(8,128)} %copy-done.1, f32[16,256]{1,0:T(8,128)S(1)} %get-tuple-element.300, ...), kind=kOutput, calls=%fused_computation.21.clone.1 | convolution fusion | flops 215416832 | bytes 14258688 | tf_op jit(solution)/shard_map/while/body/eval_jaxpr/nqk,knc->qnc/dot_general | solution.py:71
  132.8 3.8 %copy.57 = bf16[2,256,16,32]{3,2,1,0:T(8,128)(2,1)} copy(bf16[2,256,16,32]{1,3,2,0:T(8,128)(2,1)} %get-tuple-element.107) | data formatting | bytes 1048576 | tf_op jit(solution)/shard_map/while | solution.py:76
  136.6 3.6 %reshape.278 = bf16[1,2,16,16,512]{4,3,2,1,0:T(8,128)(2,1)S(1)} reshape(bf16[2,256,16,32]{3,2,1,0:T(8,128)(2,1)} %copy.57) | data formatting | bytes 1048576 | tf_op jit(solution)/shard_map/reshape | solution.py:78
  140.2 1.6 fusion.61
  141.9 2.0 fusion.49
  143.9 88.4 %all_to_all.10 = bf16[32,96,512]{2,1,0:T(8,128)(2,1)} all-to-all(bf16[32,96,512]{2,1,0:T(8,128)(2,1)S(1)} %bitcast.114), channel_id=1, replica_groups=mesh['row'=32,'col'=8] {'row'}, dimensions={0} | all-to-all | bytes 6291456 | tf_op jit(solution)/shard_map/all_to_all | solution.py:131
  232.3 18.3 %fusion.54 = bf16[32,96,512]{2,1,0:T(8,128)(2,1)} fusion(bf16[32,96,512]{2,1,0:T(8,128)(2,1)} %all_to_all.10, bf16[1,2048,512]{2,1,0:T(8,128)(2,1)S(1)} %copy-done, bf16[1,512,2048]{2,1,0:T(8,128)(2,1)} %param.20), kind=kOutput, calls=%fused_computation.52 | convolution fusion | flops 12943097856 | bytes 10485760 | tf_op jit(solution)/shard_map/secf,efd->secd/dot_general | solution.py:135
  250.7 6.0 %all-to-all-start.1 = ((bf16[32,96,512]{2,1,0:T(8,128)(2,1)}), bf16[32,96,512]{2,1,0:T(8,128)(2,1)}, u32[]{:S(2)}, u32[]{:S(2)}) async-start(bf16[32,96,512]{2,1,0:T(8,128)(2,1)} %fusion.54), calls=%async_computation.1 | async-start | bytes 6291456 | tf_op jit(solution)/shard_map/all_to_all | solution.py:139
  257.8 73.0 %all-to-all-done.1 = bf16[32,96,512]{2,1,0:T(8,128)(2,1)} async-done(((bf16[32,96,512]{2,1,0:T(8,128)(2,1)}), bf16[32,96,512]{2,1,0:T(8,128)(2,1)}, u32[]{:S(2)}, u32[]{:S(2)}) %all-to-all-start.1) | async-done | bytes 3145760 | tf_op jit(solution)/shard_map/all_to_all | solution.py:139
  330.8 6.3 %gather_fusion = bf16[1024,512]{1,0:T(8,128)(2,1)S(1)} fusion(bf16[3072,512]{1,0:T(8,128)(2,1)} %bitcast.21, s32[1024]{0:T(1024)S(1)} %broadcast_clamp_fusion), kind=kCustom, calls=%fused_computation | custom fusion | bytes 2101248 | tf_op jit(solution)/shard_map/gather | solution.py:140
  337.1 2.3 reshape.290
  339.4 4.4 %multiply_reduce_fusion = f32[512,512]{1,0:T(8,128)S(1)} fusion(f32[512,2,512]{2,1,0:T(2,128)} %reshape.290, f32[512,2]{1,0:T(8,128)S(1)} %copy.66), kind=kLoop, calls=%fused_computation.55 | loop fusion | flops 786432 | bytes 3149824 | tf_op jit(solution)/shard_map/reduce_sum | solution.py:143
  (110 shorter events, 15.4 us)
Async XLA Ops:
  0.0 232.3 %copy-start = (bf16[1,2048,512]{2,1,0:T(8,128)(2,1)S(1)}, bf16[1,2048,512]{2,1,0:T(8,128)(2,1)}, u32[]{:S(2)}) copy-start(bf16[1,2048,512]{2,1,0:T(8,128)(2,1)} %param.21) | copy-start | bytes 6291460
  2.6 12.4 %copy-start.17 = (s32[16,32]{1,0:T(8,128)S(1)}, s32[16,32]{1,0:T(8,128)}, u32[]{:S(2)}) copy-start(s32[16,32]{1,0:T(8,128)} %param.13) | copy-start | bytes 6148
  2.6 20.1 %copy-start.15 = (s32[1,1,512,2]{2,3,1,0:T(2,128)S(1)}, s32[1,1,512,2]{2,3,1,0:T(2,128)}, u32[]{:S(2)}) copy-start(s32[1,1,512,2]{2,3,1,0:T(2,128)} %param.14) | copy-start | bytes 12292
  6.7 1.2 copy-start.3
  8.8 29.9 %collective-permute-start = (bf16[6,32,1024]{2,1,0:T(8,128)(2,1)}, bf16[6,32,1024]{2,1,0:T(8,128)(2,1)S(1)}, u32[]{:S(2)}, u32[]{:S(2)}) collective-permute-start(bf16[6,32,1024]{2,1,0:T(8,128)(2,1)} %bitcast.2), channel_id=1, source_target_pairs={{0,8},{8,16},{16,24},{24,32},{32,40},{40,48},{48,56},{56,64},{64,7... | collective-permute-start | bytes 1179656 | tf_op jit(solution)/shard_map/ppermute | solution.py:19
  13.1 25.6 %collective-permute-start.1 = (bf16[6,32,1024]{2,1,0:T(8,128)(2,1)}, bf16[6,32,1024]{2,1,0:T(8,128)(2,1)}, u32[]{:S(2)}, u32[]{:S(2)}) collective-permute-start(bf16[6,32,1024]{2,1,0:T(8,128)(2,1)} %bitcast.4), channel_id=1, source_target_pairs={{8,0},{16,8},{24,16},{32,24},{40,32},{48,40},{56,48},{64,56},{72,6... | collective-permute-start | bytes 1179656 | tf_op jit(solution)/shard_map/ppermute | solution.py:21
  15.1 5.7 %copy-start.10 = (bf16[16,32]{1,0:T(8,128)(2,1)}, bf16[16,32]{1,0:T(8,128)(2,1)S(1)}, u32[]{:S(2)}) copy-start(bf16[16,32]{1,0:T(8,128)(2,1)S(1)} %convert_element_type.72) | copy-start | bytes 3076
  15.7 21.7 %collective-permute-start.4 = (bf16[6,32]{1,0:T(8,128)(2,1)}, bf16[6,32]{1,0:T(8,128)(2,1)S(1)}, u32[]{:S(2)}, u32[]{:S(2)}) collective-permute-start(bf16[6,32]{1,0:T(8,128)(2,1)} %get-tuple-element.222), channel_id=1, source_target_pairs={{0,8},{8,16},{16,24},{24,32},{32,40},{40,48},{48,56},{56,64},{64,7... | collective-permute-start | bytes 1160 | tf_op jit(solution)/shard_map/ppermute | solution.py:19
  20.8 17.2 %collective-permute-start.5 = (bf16[6,32]{1,0:T(8,128)(2,1)S(1)}, bf16[6,32]{1,0:T(8,128)(2,1)}, u32[]{:S(2)}, u32[]{:S(2)}) collective-permute-start(bf16[6,32]{1,0:T(8,128)(2,1)S(1)} %get-tuple-element.223), channel_id=1, source_target_pairs={{8,0},{16,8},{24,16},{32,24},{40,32},{48,40},{56,48},{64,56},{72,6... | collective-permute-start | bytes 1160 | tf_op jit(solution)/shard_map/ppermute | solution.py:21
  22.9 13.2 %copy-start.4 = (s32[1,1,512,2]{3,2,1,0:T(8,128)}, s32[1,1,512,2]{3,2,1,0:T(8,128)S(1)}, u32[]{:S(2)}) copy-start(s32[1,1,512,2]{3,2,1,0:T(8,128)S(1)} %copy.59) | copy-start | bytes 12292
  34.9 1.2 copy-start.13
  37.4 0.6 copy-start.19
  40.8 21.3 %collective-permute-start.2 = (bf16[28,6,1024]{2,1,0:T(8,128)(2,1)}, bf16[28,6,1024]{2,1,0:T(8,128)(2,1)}, u32[]{:S(2)}, u32[]{:S(2)}) collective-permute-start(bf16[28,6,1024]{2,1,0:T(8,128)(2,1)} %get-tuple-element.214), channel_id=1, source_target_pairs={{0,1},{1,2},{2,3},{3,4},{4,5},{5,6},{6,7},{8,9},{9,10},{10,11},{11... | collective-permute-start | bytes 1032200 | tf_op jit(solution)/shard_map/ppermute | solution.py:19
  44.0 18.1 %collective-permute-start.3 = (bf16[28,6,1024]{2,1,0:T(8,128)(2,1)}, bf16[28,6,1024]{2,1,0:T(8,128)(2,1)}, u32[]{:S(2)}, u32[]{:S(2)}) collective-permute-start(bf16[28,6,1024]{2,1,0:T(8,128)(2,1)} %get-tuple-element.215), channel_id=1, source_target_pairs={{1,0},{2,1},{3,2},{4,3},{5,4},{6,5},{7,6},{9,8},{10,9},{11,10},{12... | collective-permute-start | bytes 1032200 | tf_op jit(solution)/shard_map/ppermute | solution.py:21
  48.9 11.7 %collective-permute-start.6 = (bf16[28,6]{1,0:T(8,128)(2,1)}, bf16[28,6]{1,0:T(8,128)(2,1)S(1)}, u32[]{:S(2)}, u32[]{:S(2)}) collective-permute-start(bf16[28,6]{1,0:T(8,128)(2,1)} %get-tuple-element.218), channel_id=1, source_target_pairs={{0,1},{1,2},{2,3},{3,4},{4,5},{5,6},{6,7},{8,9},{9,10},{10,11},{11... | collective-permute-start | bytes 1016 | tf_op jit(solution)/shard_map/ppermute | solution.py:19
  50.9 10.4 %collective-permute-start.7 = (bf16[28,6]{1,0:T(8,128)(2,1)}, bf16[28,6]{1,0:T(8,128)(2,1)}, u32[]{:S(2)}, u32[]{:S(2)}) collective-permute-start(bf16[28,6]{1,0:T(8,128)(2,1)} %get-tuple-element.219), channel_id=1, source_target_pairs={{1,0},{2,1},{3,2},{4,3},{5,4},{6,5},{7,6},{9,8},{10,9},{11,10},{12... | collective-permute-start | bytes 1016 | tf_op jit(solution)/shard_map/ppermute | solution.py:21
  60.7 0.6 copy-start.18
  75.9 5.3 %copy-start.11 = (s32[256]{0:T(256)S(1)}, s32[256]{0:T(256)}, u32[]{:S(2)}) copy-start(s32[256]{0:T(256)} %get-tuple-element.341) | copy-start | bytes 3076 | tf_op jit(solution)/shard_map/while
  75.9 5.3 %copy-start.12 = (s32[256]{0:T(256)S(1)}, s32[256]{0:T(256)}, u32[]{:S(2)}) copy-start(s32[256]{0:T(256)} %get-tuple-element.339) | copy-start | bytes 3076 | tf_op jit(solution)/shard_map/while
  85.4 4.6 %copy-start.1 = (f32[16,256,784]{1,2,0:T(8,128)}, f32[16,256,784]{1,2,0:T(8,128)S(1)}, u32[]{:S(2)}) copy-start(f32[16,256,784]{1,2,0:T(8,128)S(1)} %get-tuple-element.299) | copy-start | bytes 38535172 | tf_op jit(solution)/shard_map/while
  85.4 4.6 %copy-start.2 = (bf16[784,512]{1,0:T(8,128)(2,1)S(1)}, bf16[784,512]{1,0:T(8,128)(2,1)}, u32[]{:S(2)}) copy-start(bf16[784,512]{1,0:T(8,128)(2,1)} %get-tuple-element.297) | copy-start | bytes 2408452 | tf_op jit(solution)/shard_map/while
  109.3 5.3 %copy-start.11 = (s32[256]{0:T(256)S(1)}, s32[256]{0:T(256)}, u32[]{:S(2)}) copy-start(s32[256]{0:T(256)} %get-tuple-element.341) | copy-start | bytes 3076 | tf_op jit(solution)/shard_map/while
  109.3 5.3 %copy-start.12 = (s32[256]{0:T(256)S(1)}, s32[256]{0:T(256)}, u32[]{:S(2)}) copy-start(s32[256]{0:T(256)} %get-tuple-element.339) | copy-start | bytes 3076 | tf_op jit(solution)/shard_map/while
  118.7 4.6 %copy-start.1 = (f32[16,256,784]{1,2,0:T(8,128)}, f32[16,256,784]{1,2,0:T(8,128)S(1)}, u32[]{:S(2)}) copy-start(f32[16,256,784]{1,2,0:T(8,128)S(1)} %get-tuple-element.299) | copy-start | bytes 38535172 | tf_op jit(solution)/shard_map/while
  118.7 4.6 %copy-start.2 = (bf16[784,512]{1,0:T(8,128)(2,1)S(1)}, bf16[784,512]{1,0:T(8,128)(2,1)}, u32[]{:S(2)}) copy-start(bf16[784,512]{1,0:T(8,128)(2,1)} %get-tuple-element.297) | copy-start | bytes 2408452 | tf_op jit(solution)/shard_map/while
  132.8 7.4 %copy-start.6 = (bf16[16,32,512]{2,1,0:T(8,128)(2,1)S(1)}, bf16[16,32,512]{2,1,0:T(8,128)(2,1)}, u32[]{:S(2)}) copy-start(bf16[16,32,512]{2,1,0:T(8,128)(2,1)} %param.12) | copy-start | bytes 1572868
  136.6 5.3 %copy-start.20 = (s32[512]{0:T(512)S(1)}, s32[512]{0:T(512)}, u32[]{:S(2)}) copy-start(s32[512]{0:T(512)} %get-tuple-element.188) | copy-start | bytes 6148
  136.6 5.3 %copy-start.21 = (s32[512]{0:T(512)S(1)}, s32[512]{0:T(512)}, u32[]{:S(2)}) copy-start(s32[512]{0:T(512)} %get-tuple-element.189) | copy-start | bytes 6148
  136.6 5.3 %copy-start.23 = (f32[512]{0:T(512)S(1)}, f32[512]{0:T(512)}, u32[]{:S(2)}) copy-start(f32[512]{0:T(512)} %param.18) | copy-start | bytes 6148
  141.8 2.1 copy-start.7
  250.7 6.0 %copy-start.5 = (s32[1,1,512,2]{3,2,1,0:T(8,128)S(1)}, s32[1,1,512,2]{3,2,1,0:T(8,128)}, u32[]{:S(2)}) copy-start(s32[1,1,512,2]{3,2,1,0:T(8,128)} %copy-done.4) | copy-start | bytes 12292
  250.7 6.2 %copy-start.16 = (s32[1,1,512,2]{2,3,1,0:T(2,128)S(1)}, s32[1,1,512,2]{2,3,1,0:T(2,128)}, u32[]{:S(2)}) copy-start(s32[1,1,512,2]{2,3,1,0:T(2,128)} %param.14) | copy-start | bytes 12292
  250.7 6.5 %copy-start.14 = (s32[1024]{0:T(1024)S(1)}, s32[1024]{0:T(1024)}, u32[]{:S(2)}) copy-start(s32[1024]{0:T(1024)} %copy-done.13) | copy-start | bytes 12292
  250.7 6.5 %copy-start.8 = (bf16[512,512]{1,0:T(8,128)(2,1)S(1)}, bf16[512,512]{1,0:T(8,128)(2,1)}, u32[]{:S(2)}) copy-start(bf16[512,512]{1,0:T(8,128)(2,1)} %copy-done.7) | copy-start | bytes 1572868
  250.7 6.5 %copy-start.22 = (bf16[512,32]{0,1:T(8,128)(2,1)S(1)}, bf16[512,32]{0,1:T(8,128)(2,1)}, u32[]{:S(2)}) copy-start(bf16[512,32]{0,1:T(8,128)(2,1)} %param.19) | copy-start | bytes 98308
  250.7 80.1 %all-to-all-start.1 = ((bf16[32,96,512]{2,1,0:T(8,128)(2,1)}), bf16[32,96,512]{2,1,0:T(8,128)(2,1)}, u32[]{:S(2)}, u32[]{:S(2)}) async-start(bf16[32,96,512]{2,1,0:T(8,128)(2,1)} %fusion.54), calls=%async_computation.1 | async-start | bytes 6291456 | tf_op jit(solution)/shard_map/all_to_all | solution.py:139
  339.4 4.5 %copy-start.9 = (bf16[512,512]{1,0:T(8,128)(2,1)S(1)}, bf16[512,512]{1,0:T(8,128)(2,1)}, u32[]{:S(2)}) copy-start(bf16[512,512]{1,0:T(8,128)(2,1)} %copy-done.7) | copy-start | bytes 1572868
where the time goes:
time: 346 us; the launch traced here: 345 us
  blocking collectives  88.4 us (26%)
  waiting for transfers between devices  73 us (21%)
  local copies, waits for them, and re-layouts  61.9 us (18%)
  matrix products  49.2 us (14%)
  starting transfers between devices  34.3 us (10%)
  other arithmetic  33.7 us (10%)
  loops' own time  3.91 us (1%)
    all_to_all x1, blocking collectives, per_device(): lax.all_to_all(outgoing, 'row', split_axis=0, concat_axis=0, tiled=True)  88.4 us
    all_to_all x1, waiting for transfers between devices, per_device(): back = lax.all_to_all(done, 'row', split_axis=0, concat_axis=0, tiled=True)  73 us
    dot_general x1, matrix products, per_device(): jnp.einsum('secf,efd->secd', hidden, w_down, preferred_element_type=jnp.f...  18.3 us
    dot_general x2, matrix products, one_block(): jnp.einsum('nqk,knc->qnc', weights.astype(jnp.bfloat16), values, preferre...  16.4 us
    ppermute x4, starting transfers between devices, with_halo(): lax.ppermute(tail, axis, [(i, (i + 1) % count) for i in range(ends)])  14.5 us
    ppermute x4, starting transfers between devices, with_halo(): lax.ppermute(head, axis, [((i + 1) % count, i) for i in range(ends)])  13.7 us
    another operation x2, other arithmetic  9.04 us
    dynamic_slice x2, local copies, waits for them, and re-layouts, one_block(): lax.dynamic_slice(padded, (first_row, first_col, anchor), (key_rows, key_...  7.71 us
  transfers between devices with their start and end apart: 9, of which 1 were waited for; matrix products, arithmetic and copies ran while one was open for 7% of the time, Pallas kernels for 0%

commit v1 on v0

v1 whole, which is shorter than its diff:
```python
import functools

import jax
import jax.numpy as jnp
import numpy as np
from jax import lax
from jax.experimental import pallas as pl
from jax.experimental.pallas import tpu as pltpu
from jax.sharding import Mesh, PartitionSpec as P

HEADS = 16
RADIUS = 6
CAP = 96
SIDE = 8
QROWS = 4
LANES = 128
BIG = 1e30

ROW = ("z", "xh", "core")
COL = ("xl", "y")


def norm(wide, gain):
    power = jnp.mean(wide * wide, axis=-1, keepdims=True)
    return (wide * lax.rsqrt(power + 1e-06) * gain).astype(jnp.bfloat16)


def geometry(wt):
    keyw = wt + 2 * SIDE
    krows = QROWS + 2 * RADIUS
    k = np.arange(krows * keyw)
    q = np.arange(QROWS * wt)
    kr, kc = k // keyw, k % keyw
    kc = np.where(kc < wt + SIDE, kc, kc - keyw)
    rise = kr[:, None] - q[None, :] // wt - RADIUS
    reach = kc[:, None] - q[None, :] % wt
    inside = (np.abs(rise) <= RADIUS) & (np.abs(reach) <= RADIUS)
    centre = (rise == 0) & (reach == 0)
    return (
        np.where(inside, 0.0, -BIG).astype(np.float32),
        np.where(centre, 0.0, 1.0).astype(np.float32),
    )


def attention_kernel(
    tok_ref, mask_ref, top_ref, bot_ref, left_ref, right_ref, gain_ref, wqkv_ref, wout_ref,
    gain2_ref, geo_ref, off_ref, resid_ref, moe_ref, xn, marks, keys, vals, kaug, vaug, qaug,
):
    ht, wt, width = tok_ref.shape
    keyw = wt + 2 * SIDE
    krows = QROWS + 2 * RADIUS
    slab = krows * keyw
    nq = QROWS * wt
    gain = gain_ref[...]
    step = pl.program_id(0)

    @pl.when(step == 0)
    def _prepare():
        for r in range(ht + 2 * RADIUS):
            at = r * keyw
            if r < RADIUS:
                body, mark = top_ref[r, :, :width], top_ref[r, :, width:]
            elif r < ht + RADIUS:
                body, mark = tok_ref[r - RADIUS], mask_ref[r - RADIUS]
            else:
                body = bot_ref[r - ht - RADIUS, :, :width]
                mark = bot_ref[r - ht - RADIUS, :, width:]
            xn[at : at + wt, :] = norm(body.astype(jnp.float32), gain)
            marks[at : at + wt, :] = mark.astype(jnp.float32)
            edge = jnp.concatenate(
                [right_ref[r].astype(jnp.float32), left_ref[r].astype(jnp.float32)], axis=0
            )
            xn[at + wt : at + keyw, :] = norm(edge[:, :width], gain)
            marks[at + wt : at + keyw, :] = edge[:, width:]
        every = xn[...]
        keys[...] = jnp.dot(
            every, wqkv_ref[:, width : 2 * width], preferred_element_type=jnp.float32
        ).astype(jnp.bfloat16)
        vals[...] = jnp.dot(
            every, wqkv_ref[:, 2 * width :], preferred_element_type=jnp.float32
        ).astype(jnp.bfloat16)
        vaug[:, LANES:] = jnp.ones((slab, LANES), jnp.bfloat16)
        spot = lax.broadcasted_iota(jnp.int32, (nq, nq), 0)
        lane = lax.broadcasted_iota(jnp.int32, (nq, nq), 1)
        unit = (spot == lane).astype(jnp.bfloat16)
        for i in range(4):
            qaug[i * nq : (i + 1) * nq, LANES:] = unit

    base = pl.multiple_of(step * (QROWS * keyw), QROWS * keyw)
    own = [
        xn[pl.ds(pl.multiple_of(base + (RADIUS + i) * keyw, 16), wt), :] for i in range(QROWS)
    ]
    query = jnp.dot(
        jnp.concatenate(own, axis=0), wqkv_ref[:, :width], preferred_element_type=jnp.float32
    )
    hdim = width // HEADS
    query = (query * hdim ** (-0.5)).astype(jnp.bfloat16)
    bias = geo_ref[...] + (marks[pl.ds(base, slab), :] - 1.0) * BIG * off_ref[...]
    kaug[:, LANES:] = bias.astype(jnp.bfloat16)
    per = LANES // hdim
    head_of = lax.broadcasted_iota(jnp.int32, (nq, LANES), 1) // hdim
    pieces = []
    for g in range(width // LANES):
        cols = slice(g * LANES, (g + 1) * LANES)
        qg = query[:, cols]
        for i in range(per):
            qaug[i * nq : (i + 1) * nq, :LANES] = jnp.where(head_of == i, qg, 0).astype(
                jnp.bfloat16
            )
        kaug[:, :LANES] = keys[pl.ds(base, slab), cols]
        vaug[:, :LANES] = vals[pl.ds(base, slab), cols]
        scores = lax.dot_general(
            qaug[...], kaug[...], (((1,), (1,)), ((), ())), preferred_element_type=jnp.float32
        )
        highest = jnp.max(scores, axis=-1, keepdims=True)
        weights = jnp.exp(scores - highest).astype(jnp.bfloat16)
        mixed = jnp.dot(weights, vaug[...], preferred_element_type=jnp.float32)
        share = mixed[:, :LANES] / mixed[:, LANES:]
        both = share[:nq]
        for i in range(1, per):
            both = jnp.where(head_of == i, share[i * nq : (i + 1) * nq], both)
        pieces.append(both.astype(jnp.bfloat16))
    attended = jnp.concatenate(pieces, axis=1)
    mixed = jnp.dot(attended, wout_ref[...], preferred_element_type=jnp.float32)
    mine = tok_ref[pl.ds(step * QROWS, QROWS)].reshape(nq, width)
    resid = (mine.astype(jnp.float32) + mixed).astype(jnp.bfloat16)
    resid_ref[...] = resid
    moe_ref[...] = norm(resid.astype(jnp.float32), gain2_ref[...])


def attention(tokens, marks, top, bot, left, right, gain, wqkv, wout, gain2):
    ht, wt, width = tokens.shape
    geo, off = geometry(wt)
    slab, nq = geo.shape
    total = (ht + 2 * RADIUS) * (wt + 2 * SIDE)
    whole = lambda a: pl.BlockSpec(a.shape, functools.partial(lambda n, i: (0,) * n, a.ndim))
    args = (
        tokens, marks, top, bot, left, right, gain.reshape(1, width), wqkv, wout,
        gain2.reshape(1, width), jnp.asarray(geo), jnp.asarray(off),
    )
    out = jax.ShapeDtypeStruct((ht * wt, width), jnp.bfloat16)
    bf = jnp.bfloat16
    return pl.pallas_call(
        attention_kernel,
        grid=(ht // QROWS,),
        in_specs=[whole(a) for a in args],
        out_specs=[pl.BlockSpec((nq, width), lambda i: (i, 0))] * 2,
        out_shape=[out, out],
        scratch_shapes=[
            pltpu.VMEM((total, width), bf),
            pltpu.VMEM((total, LANES), jnp.float32),
            pltpu.VMEM((total, width), bf),
            pltpu.VMEM((total, width), bf),
            pltpu.VMEM((slab, 2 * LANES), bf),
            pltpu.VMEM((slab, 2 * LANES), bf),
            pltpu.VMEM((4 * nq, 2 * LANES), bf),
        ],
        compiler_params=pltpu.CompilerParams(vmem_limit_bytes=48 << 20),
        cost_estimate=pl.CostEstimate(
            flops=10_000_000_000, bytes_accessed=6_000_000, transcendentals=6_000_000
        ),
    )(*args)


def halo(tokens, mask):
    ht, wt, width = tokens.shape
    count = lax.axis_size(ROW)
    across = lax.axis_size(COL)
    ahead = lambda n: [(i, i + 1) for i in range(n - 1)]
    back = lambda n: [(i + 1, i) for i in range(n - 1)]
    marks = jnp.broadcast_to(mask.astype(jnp.bfloat16)[..., None], (ht, wt, LANES))
    both = lambda rows: jnp.concatenate([tokens[rows], marks[rows]], axis=-1)
    top = lax.ppermute(both(slice(ht - RADIUS, ht)), ROW, ahead(count))
    bot = lax.ppermute(both(slice(0, RADIUS)), ROW, back(count))

    def edge(cols):
        mine = jnp.concatenate([tokens[:, cols], marks[:, cols]], axis=-1)
        return jnp.concatenate([top[:, cols], mine, bot[:, cols]], axis=0)

    left = lax.ppermute(edge(slice(wt - SIDE, wt)), COL, ahead(across))
    right = lax.ppermute(edge(slice(0, SIDE)), COL, back(across))
    return marks, top, bot, left, right


def experts_kernel(
    who_ref, ids_ref, x0, f1, f2, f3, f4, b4, b3, b2, b1, wr_ref, *refs
):
    w_in, w_down = refs[0:4], refs[4:8]
    outs = refs[8:16]
    rows, share, done, acc, buf_in, buf_down, sem = refs[16:]
    half = f4.shape[0]
    patches, width = x0.shape
    ff = w_in[0].shape[-1]
    chunk = buf_in.shape[-1]
    chunks = ff // chunk
    steps = 4 * chunks
    me = who_ref[0]
    z = me // 4

    def copies(n):
        j, c = n // chunks, n % chunks
        slot = n % 2
        span = pl.ds(c * chunk, chunk)
        return (
            pltpu.make_async_copy(w_in[j].at[:, span], buf_in.at[slot], sem.at[slot, 0]),
            pltpu.make_async_copy(w_down[j].at[span, :], buf_down.at[slot], sem.at[slot, 1]),
        )

    for c in copies(0):
        c.start()
    before = lax.broadcasted_iota(jnp.int32, (patches, patches), 0)
    after = lax.broadcasted_iota(jnp.int32, (patches, patches), 1)
    upper = (before < after).astype(jnp.bfloat16)
    slot_of = lax.broadcasted_iota(jnp.int32, (CAP, patches), 0).astype(jnp.float32)
    held = [me ^ j for j in range(4)]
    lane_expert = lax.broadcasted_iota(jnp.int32, (wr_ref.shape[0], patches), 0)
    for d in range(8):
        ids = ids_ref[(z + 8 - d) % 8]
        e0, e1 = ids[0:1], ids[1:2]
        if d == 4:
            x = jnp.concatenate([f4[...], b4[...]], axis=0)
        else:
            x = (x0, f1, f2, f3, None, b3, b2, b1)[d][...]
        logits = lax.dot_general(
            wr_ref[...], x, (((1,), (1,)), ((), ())), preferred_element_type=jnp.float32
        )
        pick = lambda e: jnp.sum(jnp.where(lane_expert == e, logits, 0.0), axis=0, keepdims=True)
        gap = pick(e0) - pick(e1)
        g0, g1 = jax.nn.sigmoid(gap), jax.nn.sigmoid(-gap)
        named = [((e0 == h) | (e1 == h)).astype(jnp.float32) for h in held]
        hot = jnp.concatenate(named + named, axis=0)
        rank = jnp.dot(hot.astype(jnp.bfloat16), upper, preferred_element_type=jnp.float32)
        for j in range(4):
            place = jnp.where(named[j] > 0.5, rank[j : j + 1], -1.0)
            hit = slot_of == place
            gate = jnp.where(e0 == held[j], g0, g1)
            share[d, j * CAP : (j + 1) * CAP, :] = jnp.where(hit, gate, 0.0).astype(jnp.bfloat16)
            one = hit.astype(jnp.float32).astype(jnp.bfloat16)
            rows[j, d * CAP : (d + 1) * CAP, :] = jnp.dot(
                one, x, preferred_element_type=jnp.float32
            ).astype(jnp.bfloat16)
    for n in range(steps):
        j, c = n // chunks, n % chunks
        if n + 1 < steps:
            for cp in copies(n + 1):
                cp.start()
        for cp in copies(n):
            cp.wait()
        hidden = jnp.dot(rows[j], buf_in[n % 2], preferred_element_type=jnp.float32)
        hidden = jax.nn.gelu(hidden, approximate=True).astype(jnp.bfloat16)
        part = jnp.dot(hidden, buf_down[n % 2], preferred_element_type=jnp.float32)
        if c == 0:
            acc[...] = part
        elif c < chunks - 1:
            acc[...] += part
        else:
            whole = (acc[...] + part).astype(jnp.bfloat16)
            for d in range(8):
                done[d, j * CAP : (j + 1) * CAP, :] = whole[d * CAP : (d + 1) * CAP]
    for d in range(8):
        outs[d][...] = lax.dot_general(
            share[d], done[d], (((0,), (0,)), ((), ())), preferred_element_type=jnp.float32
        ).astype(jnp.bfloat16)


def experts(who, ids, blocks, router, w_in, w_down):
    patches, width = blocks[0].shape
    ff = w_in[0].shape[-1]
    chunk = 512
    vm = pl.BlockSpec(memory_space=pltpu.VMEM)
    hbm = pl.BlockSpec(memory_space=pl.ANY)
    bf = jnp.bfloat16
    return pl.pallas_call(
        experts_kernel,
        in_specs=[pl.BlockSpec(memory_space=pltpu.SMEM)] + [vm] * 11 + [hbm] * 8,
        out_specs=[vm] * 8,
        out_shape=[jax.ShapeDtypeStruct((patches, width), bf)] * 8,
        scratch_shapes=[
            pltpu.VMEM((4, 8 * CAP, width), bf),
            pltpu.VMEM((8, 4 * CAP, patches), bf),
            pltpu.VMEM((8, 4 * CAP, width), bf),
            pltpu.VMEM((8 * CAP, width), jnp.float32),
            pltpu.VMEM((2, width, chunk), bf),
            pltpu.VMEM((2, chunk, width), bf),
            pltpu.SemaphoreType.DMA((2, 2)),
        ],
        compiler_params=pltpu.CompilerParams(vmem_limit_bytes=56 << 20),
        cost_estimate=pl.CostEstimate(
            flops=16_000_000_000, bytes_accessed=26_000_000, transcendentals=6_000_000
        ),
    )(who, ids, *blocks, router, *w_in, *w_down)


def around(step):
    count = lax.axis_size("z")
    return [(i, (i + step) % count) for i in range(count)]


def spread(x):
    half = x.shape[0] // 2
    ahead, back = around(1), around(-1)
    f, b = [x], [x]
    for _ in range(3):
        f.append(lax.ppermute(f[-1], "z", ahead))
        b.append(lax.ppermute(b[-1], "z", back))
    f4 = lax.ppermute(f[-1][:half], "z", ahead)
    b4 = lax.ppermute(b[-1][half:], "z", back)
    return x, f[1], f[2], f[3], f4, b4, b[3], b[2], b[1]


def collect(parts):
    half = parts[0].shape[0] // 2
    lo, hi = slice(0, half), slice(half, 2 * half)
    ahead, back = around(1), around(-1)

    def add(a, b):
        return (a.astype(jnp.float32) + b.astype(jnp.float32)).astype(jnp.bfloat16)

    f0 = lax.ppermute(parts[4][lo], "z", back)
    b1 = lax.ppermute(parts[4][hi], "z", ahead)
    f1 = lax.ppermute(parts[3][hi], "z", back)
    b0 = lax.ppermute(parts[5][lo], "z", ahead)
    for i in (3, 2, 1):
        f0 = lax.ppermute(add(f0, parts[i][lo]), "z", back)
        b1 = lax.ppermute(add(b1, parts[8 - i][hi]), "z", ahead)
        if i > 1:
            f1 = lax.ppermute(add(f1, parts[i - 1][hi]), "z", back)
            b0 = lax.ppermute(add(b0, parts[9 - i][lo]), "z", ahead)
    return jnp.concatenate(
        [f0.astype(jnp.float32) + b0.astype(jnp.float32), f1.astype(jnp.float32) + b1.astype(jnp.float32)],
        axis=0,
    )


def plane_weights(w):
    rows = w.shape[0]
    across = lax.axis_size(COL)
    piece = rows // across
    col = lax.axis_index(COL)
    per = across // 2
    want = (col + per) % across
    part = lax.dynamic_slice_in_dim(w, want * piece, piece, 0)
    part = lax.ppermute(part, ("xh", "xl"), [(0, 3), (3, 0), (1, 2), (2, 1)])
    far = lax.all_gather(part, COL, axis=0, tiled=True)
    swap = [(0, 1), (1, 0)]
    return w, lax.ppermute(w, "core", swap), far, lax.ppermute(far, "core", swap)


def per_device(
    tokens, die_mask, expert_ids, gain_attn, w_qkv, w_out, gain_moe, w_router, w_in, w_down
):
    ht, wt, width = tokens.shape
    patches = ht * wt
    marks, top, bot, left, right = halo(tokens, die_mask)
    ids = lax.all_gather(expert_ids.reshape(patches, 2).T, "z", axis=0)
    w_ins = plane_weights(w_in.reshape(w_in.shape[1:]))
    w_downs = plane_weights(w_down.reshape(w_down.shape[1:]))
    resid, normed_moe = attention(
        tokens, marks, top, bot, left, right, gain_attn, w_qkv, w_out, gain_moe
    )
    blocks = spread(normed_moe)
    who = lax.axis_index(ROW).reshape(1).astype(jnp.int32)
    parts = experts(who, ids, blocks, w_router.T, w_ins, w_downs)
    moe = parts[0].astype(jnp.float32) + collect(parts)
    final = (resid.astype(jnp.float32) + moe).astype(jnp.bfloat16)
    return final.reshape(ht, wt, width)


def solution(mesh):
    fine = Mesh(mesh.devices.reshape(8, 2, 2, 2, 4), ROW + COL)
    return jax.shard_map(
        per_device,
        mesh=fine,
        in_specs=(
            P(ROW, COL, None),
            P(ROW, COL),
            P(ROW, COL, None, None),
            P(),
            P(),
            P(),
            P(),
            P(),
            P(ROW, None, None),
            P(ROW, None, None),
        ),
        out_specs=P(ROW, COL, None),
        check_vma=False,
    )
```

time: 346 us -> 295 us (0.85)
  the two profiles are of different devices: /device:TPU:3 before, /device:TPU:4 now
where the time goes in v1:
time: 295 us; the launch traced here: 290 us
  waiting for transfers between devices  130 us (44%)
  starting transfers between devices  53.4 us (18%)
  Pallas kernels  53.3 us (18%)
  blocking collectives  27.5 us (9%)
  between operations  14.2 us (5%)
  local copies, waits for them, and re-layouts  8.15 us (3%)
  other arithmetic  3.59 us (1%)
    pallas_call x1, Pallas kernels, experts(): pl.pallas_call(experts_kernel, in_specs=[pl.BlockSpec(memory_space=pltpu....  38.8 us
    ppermute x3, waiting for transfers between devices, spread(): f.append(lax.ppermute(f[-1], 'z', ahead))  28.8 us
    all_gather x1, blocking collectives, per_device(): ids = lax.all_gather(expert_ids.reshape(patches, 2).T, 'z', axis=0)  27.5 us
    all_gather x2, waiting for transfers between devices, plane_weights(): far = lax.all_gather(part, COL, axis=0, tiled=True)  20.7 us
    ppermute x3, waiting for transfers between devices, spread(): b.append(lax.ppermute(b[-1], 'z', back))  20.1 us
    ppermute x3, starting transfers between devices, spread(): b.append(lax.ppermute(b[-1], 'z', back))  16.9 us
    pallas_call x1, Pallas kernels, attention(): pl.pallas_call(attention_kernel, grid=(ht // QROWS,), in_specs=[whole(a)...  14.5 us
    ppermute x2, waiting for transfers between devices, plane_weights(): part = lax.ppermute(part, ('xh', 'xl'), [(0, 3), (3, 0), (1, 2), (2, 1)])  13.4 us
  transfers between devices with their start and end apart: 34, of which 23 were waited for; matrix products, arithmetic and copies ran while one was open for 2% of the time, Pallas kernels for 5%

profile of v1, /device:TPU:4, one launch (start us, length us, event | category | flops | bytes accessed | tf_op | source)
XLA Modules:
  0.0 290.2 jit_solution(9780520445840829537)
XLA Ops:
  6.5 1.0 dynamic-slice_bitcast_fusion.1
  8.2 7.5 %collective-permute-done.13 = bf16[64,2048]{1,0:T(8,128)(2,1)S(1)} collective-permute-done((bf16[64,2048]{1,0:T(8,128)(2,1)S(1)}, bf16[64,2048]{1,0:T(8,128)(2,1)S(1)}, u32[]{:S(2)}, u32[]{:S(2)}) %collective-permute-start.13) | collective-permute-done | bytes 262176 | tf_op jit(solution)/shard_map/ppermute | solution.py:343
  16.5 1.0 dynamic-slice_bitcast_fusion
  18.8 5.9 %collective-permute-done.16 = bf16[256,512]{1,0:T(8,128)(2,1)S(1)} collective-permute-done((bf16[256,512]{1,0:T(8,128)(2,1)S(1)}, bf16[256,512]{1,0:T(8,128)(2,1)S(1)}, u32[]{:S(2)}, u32[]{:S(2)}) %collective-permute-start.16) | collective-permute-done | bytes 262176 | tf_op jit(solution)/shard_map/ppermute | solution.py:343
  24.7 0.7 copy-done.15
  25.5 1.2 fusion.4
  26.9 1.9 collective-permute-start
  28.9 5.1 %collective-permute-start.1 = (bf16[6,32,640]{2,1,0:T(8,128)(2,1)S(1)}, bf16[6,32,640]{2,1,0:T(8,128)(2,1)S(1)}, u32[]{:S(2)}, u32[]{:S(2)}) collective-permute-start(bf16[6,32,640]{2,1,0:T(8,128)(2,1)S(1)} %pad_maximum_fusion.3), channel_id=1, source_target_pairs={{8,0},{16,8},{24,16},{32,24},{40,32},{48,40},{56,48},{64,56},{72,6... | collective-permute-start | bytes 737288 | tf_op jit(solution)/shard_map/ppermute | solution.py:174
  34.2 3.7 %collective-permute-done.top_ref = bf16[6,32,640]{2,1,0:T(8,128)(2,1)S(1)} collective-permute-done((bf16[6,32,640]{2,1,0:T(8,128)(2,1)S(1)}, bf16[6,32,640]{2,1,0:T(8,128)(2,1)S(1)}, u32[]{:S(2)}, u32[]{:S(2)}) %collective-permute-start) | collective-permute-done | bytes 245792 | tf_op jit(solution)/shard_map/ppermute | solution.py:173
  37.9 1.4 collective-permute-done.1.bot_ref
  39.4 2.0 collective-permute-start.2
  41.5 1.3 collective-permute-start.3
  42.8 5.8 %collective-permute-done.2.left_ref = bf16[28,8,640]{2,1,0:T(8,128)(2,1)S(1)} collective-permute-done((bf16[28,8,640]{2,1,0:T(8,128)(2,1)S(1)}, bf16[28,8,640]{2,1,0:T(8,128)(2,1)S(1)}, u32[]{:S(2)}, u32[]{:S(2)}) %collective-permute-start.2) | collective-permute-done | bytes 286752 | tf_op jit(solution)/shard_map/ppermute | solution.py:180
  48.6 4.8 %collective-permute-done.3.right_ref = bf16[28,8,640]{2,1,0:T(8,128)(2,1)S(1)} collective-permute-done((bf16[28,8,640]{2,1,0:T(8,128)(2,1)S(1)}, bf16[28,8,640]{2,1,0:T(8,128)(2,1)S(1)}, u32[]{:S(2)}, u32[]{:S(2)}) %collective-permute-start.3) | collective-permute-done | bytes 286752 | tf_op jit(solution)/shard_map/ppermute | solution.py:181
  53.6 14.5 %shard_map.118 = (bf16[512,512]{1,0:T(8,128)(2,1)S(1)}, bf16[512,512]{1,0:T(8,128)(2,1)S(1)}) custom-call(bf16[16,32,512]{2,1,0:T(8,128)(2,1)S(1)} %copy-done, bf16[16,32,128]{2,1,0:T(8,128)(2,1)S(1)} %broadcast_in_dim.14.mask_ref, bf16[6,32,640]{2,1,0:T(8,128)(2,1)S(1)} %collective-permute-done.top_ref, ...), custom_call_target="tpu_custom_call" | custom-call | flops 10000000000 | bytes 6000000 | tf_op jit(solution)/shard_map/pallas_call | solution.py:143
  68.2 10.0 %collective-permute-start.8 = (bf16[512,512]{1,0:T(8,128)(2,1)S(1)}, bf16[512,512]{1,0:T(8,128)(2,1)S(1)}, u32[]{:S(2)}, u32[]{:S(2)}) collective-permute-start(bf16[512,512]{1,0:T(8,128)(2,1)S(1)} %get-tuple-element.16.x0), channel_id=1, source_target_pairs={{0,224},{32,0},{64,32},{96,64},{128,96},{160,128},{192,160},{224,1... | collective-permute-start | bytes 1572872 | tf_op jit(solution)/shard_map/ppermute | solution.py:305
  78.2 8.2 %collective-permute-done.8.b1 = bf16[512,512]{1,0:T(8,128)(2,1)S(1)} collective-permute-done((bf16[512,512]{1,0:T(8,128)(2,1)S(1)}, bf16[512,512]{1,0:T(8,128)(2,1)S(1)}, u32[]{:S(2)}, u32[]{:S(2)}) %collective-permute-start.8) | collective-permute-done | bytes 524320 | tf_op jit(solution)/shard_map/ppermute | solution.py:305
  86.4 4.9 %collective-permute-start.9 = (bf16[512,512]{1,0:T(8,128)(2,1)S(1)}, bf16[512,512]{1,0:T(8,128)(2,1)S(1)}, u32[]{:S(2)}, u32[]{:S(2)}) collective-permute-start(bf16[512,512]{1,0:T(8,128)(2,1)S(1)} %collective-permute-done.8.b1), channel_id=1, source_target_pairs={{0,224},{32,0},{64,32},{96,64},{128,96},{160,128},{192,160},{224,1... | collective-permute-start | bytes 1572872 | tf_op jit(solution)/shard_map/ppermute | solution.py:305
  91.2 1.4 collective-permute-start.12
  93.7 20.7 %all-gather.7.cloned.1.call-done.refs_6_ = bf16[2048,512]{1,0:T(8,128)(2,1)} async-done(((bf16[256,512]{1,0:T(8,128)(2,1)}), bf16[2048,512]{1,0:T(8,128)(2,1)}) %all-gather.7.cloned.1.call-update) | async-done | bytes 2097168 | tf_op jit(solution)/shard_map/all_gather | solution.py:344
  114.4 1.6 collective-permute-start.5
  116.0 14.3 %collective-permute-done.5.f2 = bf16[512,512]{1,0:T(8,128)(2,1)S(1)} collective-permute-done((bf16[512,512]{1,0:T(8,128)(2,1)S(1)}, bf16[512,512]{1,0:T(8,128)(2,1)S(1)}, u32[]{:S(2)}, u32[]{:S(2)}) %collective-permute-start.5) | collective-permute-done | bytes 524320 | tf_op jit(solution)/shard_map/ppermute | solution.py:304
  130.3 2.0 collective-permute-start.10
  132.3 11.9 %collective-permute-done.10.b3 = bf16[512,512]{1,0:T(8,128)(2,1)S(1)} collective-permute-done((bf16[512,512]{1,0:T(8,128)(2,1)S(1)}, bf16[512,512]{1,0:T(8,128)(2,1)S(1)}, u32[]{:S(2)}, u32[]{:S(2)}) %collective-permute-start.10) | collective-permute-done | bytes 524320 | tf_op jit(solution)/shard_map/ppermute | solution.py:305
  144.3 14.0 %collective-permute-done.6.f3 = bf16[512,512]{1,0:T(8,128)(2,1)S(1)} collective-permute-done((bf16[512,512]{1,0:T(8,128)(2,1)S(1)}, bf16[512,512]{1,0:T(8,128)(2,1)S(1)}, u32[]{:S(2)}, u32[]{:S(2)}) %collective-permute-start.6) | collective-permute-done | bytes 524320 | tf_op jit(solution)/shard_map/ppermute | solution.py:304
  158.3 1.3 collective-permute-start.11
  159.6 0.8 collective-permute-start.7
  160.5 27.5 %all-gather.1.ids_ref = s32[8,2,512]{2,1,0:T(2,128)} all-gather(s32[1,2,512]{2,1,0:T(2,128)S(1)} %bitcast.18), channel_id=2, replica_groups=mesh['z'=8,'xh'=2,'core'=2,'xl'=2,'y'=4] {'z'}, dimensions={0}, use_global_device_ids=true | all-gather | bytes 36864 | tf_op jit(solution)/shard_map/all_gather | solution.py:355
  188.7 38.8 %shard_map.119 = (bf16[512,512]{1,0:T(8,128)(2,1)}, bf16[512,512]{1,0:T(8,128)(2,1)}, bf16[512,512]{1,0:T(8,128)(2,1)}, bf16[512,512]{1,0:T(8,128)(2,1)}, bf16[5...) custom-call(s32[1]{0:T(128)} %bitcast.2.who_ref, ...), custom_call_target="tpu_custom_call" | custom-call | flops 16000000000 | bytes 26000000 | tf_op jit(solution)/shard_map/pallas_call | solution.py:273
  227.6 1.2 fusion.2
  228.7 1.2 collective-permute-start.18
  229.9 0.9 collective-permute-start.28
  230.8 1.0 slice.109
  231.8 2.4 collective-permute-start.25
  234.2 0.9 collective-permute-done.18
  235.2 1.0 add_convert_fusion.9
  236.2 3.4 %collective-permute-start.19 = (bf16[256,512]{1,0:T(8,128)(2,1)S(1)}, bf16[256,512]{1,0:T(8,128)(2,1)S(1)}, u32[]{:S(2)}, u32[]{:S(2)}) collective-permute-start(bf16[256,512]{1,0:T(8,128)(2,1)S(1)} %add_convert_fusion.9), channel_id=1, source_target_pairs={{0,224},{32,0},{64,32},{96,64},{128,96},{160,128},{192,160},{224,1... | collective-permute-start | bytes 786440 | tf_op jit(solution)/shard_map/ppermute | solution.py:324
  240.8 5.6 %collective-permute-done.19 = bf16[256,512]{1,0:T(8,128)(2,1)S(1)} collective-permute-done((bf16[256,512]{1,0:T(8,128)(2,1)S(1)}, bf16[256,512]{1,0:T(8,128)(2,1)S(1)}, u32[]{:S(2)}, u32[]{:S(2)}) %collective-permute-start.19) | collective-permute-done | bytes 262176 | tf_op jit(solution)/shard_map/ppermute | solution.py:324
  246.6 3.6 %collective-permute-start.20 = (bf16[256,512]{1,0:T(8,128)(2,1)S(1)}, bf16[256,512]{1,0:T(8,128)(2,1)S(1)}, u32[]{:S(2)}, u32[]{:S(2)}) collective-permute-start(bf16[256,512]{1,0:T(8,128)(2,1)S(1)} %get-tuple-element.27), channel_id=1, source_target_pairs={{0,224},{32,0},{64,32},{96,64},{128,96},{160,128},{192,160},{224,1... | collective-permute-start | bytes 786440 | tf_op jit(solution)/shard_map/ppermute | solution.py:324
  250.3 5.1 %collective-permute-done.29 = bf16[256,512]{1,0:T(8,128)(2,1)S(1)} collective-permute-done((bf16[256,512]{1,0:T(8,128)(2,1)S(1)}, bf16[256,512]{1,0:T(8,128)(2,1)S(1)}, u32[]{:S(2)}, u32[]{:S(2)}) %collective-permute-start.29) | collective-permute-done | bytes 262176 | tf_op jit(solution)/shard_map/ppermute | solution.py:325
  256.1 2.8 collective-permute-done.26
  259.0 3.8 %collective-permute-start.21 = (bf16[256,512]{1,0:T(8,128)(2,1)S(1)}, bf16[256,512]{1,0:T(8,128)(2,1)S(1)}, u32[]{:S(2)}, u32[]{:S(2)}) collective-permute-start(bf16[256,512]{1,0:T(8,128)(2,1)S(1)} %get-tuple-element.25), channel_id=1, source_target_pairs={{0,224},{32,0},{64,32},{96,64},{128,96},{160,128},{192,160},{224,1... | collective-permute-start | bytes 786440 | tf_op jit(solution)/shard_map/ppermute | solution.py:324
  262.8 3.2 %collective-permute-done.23 = bf16[256,512]{1,0:T(8,128)(2,1)S(1)} collective-permute-done((bf16[256,512]{1,0:T(8,128)(2,1)S(1)}, bf16[256,512]{1,0:T(8,128)(2,1)S(1)}, u32[]{:S(2)}, u32[]{:S(2)}) %collective-permute-start.23) | collective-permute-done | bytes 262176 | tf_op jit(solution)/shard_map/ppermute | solution.py:328
  266.0 4.9 %collective-permute-done.30 = bf16[256,512]{1,0:T(8,128)(2,1)S(1)} collective-permute-done((bf16[256,512]{1,0:T(8,128)(2,1)S(1)}, bf16[256,512]{1,0:T(8,128)(2,1)S(1)}, u32[]{:S(2)}, u32[]{:S(2)}) %collective-permute-start.30) | collective-permute-done | bytes 262176 | tf_op jit(solution)/shard_map/ppermute | solution.py:325
  271.2 3.2 %collective-permute-start.27 = (bf16[256,512]{1,0:T(8,128)(2,1)S(1)}, bf16[256,512]{1,0:T(8,128)(2,1)S(1)}, u32[]{:S(2)}, u32[]{:S(2)}) collective-permute-start(bf16[256,512]{1,0:T(8,128)(2,1)S(1)} %get-tuple-element.26), channel_id=1, source_target_pairs={{0,224},{32,0},{64,32},{96,64},{128,96},{160,128},{192,160},{224,1... | collective-permute-start | bytes 786440 | tf_op jit(solution)/shard_map/ppermute | solution.py:327
  274.4 4.3 %collective-permute-done.24 = bf16[256,512]{1,0:T(8,128)(2,1)S(1)} collective-permute-done((bf16[256,512]{1,0:T(8,128)(2,1)S(1)}, bf16[256,512]{1,0:T(8,128)(2,1)S(1)}, u32[]{:S(2)}, u32[]{:S(2)}) %collective-permute-start.24) | collective-permute-done | bytes 262176 | tf_op jit(solution)/shard_map/ppermute | solution.py:328
  278.9 3.2 %collective-permute-done.31 = bf16[256,512]{1,0:T(8,128)(2,1)S(1)} collective-permute-done((bf16[256,512]{1,0:T(8,128)(2,1)S(1)}, bf16[256,512]{1,0:T(8,128)(2,1)S(1)}, u32[]{:S(2)}, u32[]{:S(2)}) %collective-permute-start.31) | collective-permute-done | bytes 262176 | tf_op jit(solution)/shard_map/ppermute | solution.py:325
  282.1 1.0 fusion.1
  (105 shorter events, 7.8 us)
Async XLA Ops:
  6.5 27.5 %copy-start = (bf16[16,32,512]{2,1,0:T(8,128)(2,1)S(1)}, bf16[16,32,512]{2,1,0:T(8,128)(2,1)}, u32[]{:S(2)}) copy-start(bf16[16,32,512]{2,1,0:T(8,128)(2,1)} %tok_ref.1) | copy-start | bytes 1572868
  6.5 86.1 %all-gather.5.cloned.1.call-start = ((), (), s32[]{:S(2)}) async-start(), calls=%async_computation | async-start | bytes 2359296 | tf_op jit(solution)/shard_map/all_gather | solution.py:344
  7.6 8.1 %collective-permute-start.13 = (bf16[64,2048]{1,0:T(8,128)(2,1)S(1)}, bf16[64,2048]{1,0:T(8,128)(2,1)S(1)}, u32[]{:S(2)}, u32[]{:S(2)}) collective-permute-start(bf16[64,2048]{1,0:T(8,128)(2,1)S(1)} %dynamic-slice_bitcast_fusion.1), channel_id=1, source_target_pairs={{0,20},{20,0},{4,16},{16,4},{1,21},{21,1},{5,17},{17,5},{2,22},{22... | collective-permute-start | bytes 786440 | tf_op jit(solution)/shard_map/ppermute | solution.py:343
  16.4 98.0 %all-gather.7.cloned.1.call-start = ((), (), s32[]{:S(2)}) async-start(), calls=%async_computation.1 | async-start | bytes 2359296 | tf_op jit(solution)/shard_map/all_gather | solution.py:344
  17.5 7.3 %collective-permute-start.16 = (bf16[256,512]{1,0:T(8,128)(2,1)S(1)}, bf16[256,512]{1,0:T(8,128)(2,1)S(1)}, u32[]{:S(2)}, u32[]{:S(2)}) collective-permute-start(bf16[256,512]{1,0:T(8,128)(2,1)S(1)} %dynamic-slice_bitcast_fusion), channel_id=1, source_target_pairs={{0,20},{20,0},{4,16},{16,4},{1,21},{21,1},{5,17},{17,5},{2,22},{22... | collective-permute-start | bytes 786440 | tf_op jit(solution)/shard_map/ppermute | solution.py:343
  25.5 28.1 %copy-start.1 = (bf16[512,1536]{1,0:T(8,128)(2,1)S(1)}, bf16[512,1536]{1,0:T(8,128)(2,1)}, u32[]{:S(2)}) copy-start(bf16[512,1536]{1,0:T(8,128)(2,1)} %wqkv_ref.1) | copy-start | bytes 4718596
  25.5 28.1 %copy-start.2 = (bf16[512,512]{1,0:T(8,128)(2,1)S(1)}, bf16[512,512]{1,0:T(8,128)(2,1)}, u32[]{:S(2)}) copy-start(bf16[512,512]{1,0:T(8,128)(2,1)} %wout_ref.1) | copy-start | bytes 1572868
  25.5 28.1 %copy-start.4 = (f32[512]{0:T(512)S(1)}, f32[512]{0:T(512)}, u32[]{:S(2)}) copy-start(f32[512]{0:T(512)} %param.15) | copy-start | bytes 6148
  25.5 28.1 %copy-start.5 = (f32[512]{0:T(512)S(1)}, f32[512]{0:T(512)}, u32[]{:S(2)}) copy-start(f32[512]{0:T(512)} %param.18) | copy-start | bytes 6148
  25.5 28.1 %copy-start.6 = (f32[768,128]{1,0:T(8,128)S(1)}, f32[768,128]{1,0:T(8,128)}, u32[]{:S(2)}) copy-start(f32[768,128]{1,0:T(8,128)} %constant.56.clone.off_ref) | copy-start | bytes 1179652
  25.5 28.1 %copy-start.7 = (f32[768,128]{1,0:T(8,128)S(1)}, f32[768,128]{1,0:T(8,128)}, u32[]{:S(2)}) copy-start(f32[768,128]{1,0:T(8,128)} %constant.55.clone.geo_ref) | copy-start | bytes 1179652
  26.9 11.0 %collective-permute-start = (bf16[6,32,640]{2,1,0:T(8,128)(2,1)S(1)}, bf16[6,32,640]{2,1,0:T(8,128)(2,1)S(1)}, u32[]{:S(2)}, u32[]{:S(2)}) collective-permute-start(bf16[6,32,640]{2,1,0:T(8,128)(2,1)S(1)} %pad_maximum_fusion.2), channel_id=1, source_target_pairs={{0,8},{8,16},{16,24},{24,32},{32,40},{40,48},{48,56},{56,64},{64,7... | collective-permute-start | bytes 737288 | tf_op jit(solution)/shard_map/ppermute | solution.py:173
  28.9 10.4 %collective-permute-start.1 = (bf16[6,32,640]{2,1,0:T(8,128)(2,1)S(1)}, bf16[6,32,640]{2,1,0:T(8,128)(2,1)S(1)}, u32[]{:S(2)}, u32[]{:S(2)}) collective-permute-start(bf16[6,32,640]{2,1,0:T(8,128)(2,1)S(1)} %pad_maximum_fusion.3), channel_id=1, source_target_pairs={{8,0},{16,8},{24,16},{32,24},{40,32},{48,40},{56,48},{64,56},{72,6... | collective-permute-start | bytes 737288 | tf_op jit(solution)/shard_map/ppermute | solution.py:174
  39.4 9.2 %collective-permute-start.2 = (bf16[28,8,640]{2,1,0:T(8,128)(2,1)S(1)}, bf16[28,8,640]{2,1,0:T(8,128)(2,1)S(1)}, u32[]{:S(2)}, u32[]{:S(2)}) collective-permute-start(bf16[28,8,640]{2,1,0:T(8,128)(2,1)S(1)} %pad_maximum_fusion), channel_id=1, source_target_pairs={{0,1},{1,2},{2,3},{3,4},{4,5},{5,6},{6,7},{8,9},{9,10},{10,11},{11... | collective-permute-start | bytes 860168 | tf_op jit(solution)/shard_map/ppermute | solution.py:180
  41.5 11.9 %collective-permute-start.3 = (bf16[28,8,640]{2,1,0:T(8,128)(2,1)S(1)}, bf16[28,8,640]{2,1,0:T(8,128)(2,1)S(1)}, u32[]{:S(2)}, u32[]{:S(2)}) collective-permute-start(bf16[28,8,640]{2,1,0:T(8,128)(2,1)S(1)} %pad_maximum_fusion.1), channel_id=1, source_target_pairs={{1,0},{2,1},{3,2},{4,3},{5,4},{6,5},{7,6},{9,8},{10,9},{11,10},{12... | collective-permute-start | bytes 860168 | tf_op jit(solution)/shard_map/ppermute | solution.py:181
  53.6 106.8 %copy-start.18 = (s32[1,1,512,2]{2,3,1,0:T(2,128)S(1)}, s32[1,1,512,2]{2,3,1,0:T(2,128)}, u32[]{:S(2)}) copy-start(s32[1,1,512,2]{2,3,1,0:T(2,128)} %param.14) | copy-start | bytes 12292
  68.1 119.9 %copy-start.3 = (bf16[512,512]{1,0:T(8,128)(2,1)}, bf16[512,512]{1,0:T(8,128)(2,1)S(1)}, u32[]{:S(2)}) copy-start(bf16[512,512]{1,0:T(8,128)(2,1)S(1)} %get-tuple-element.16.x0) | copy-start | bytes 1572868
  68.2 18.2 %collective-permute-start.8 = (bf16[512,512]{1,0:T(8,128)(2,1)S(1)}, bf16[512,512]{1,0:T(8,128)(2,1)S(1)}, u32[]{:S(2)}, u32[]{:S(2)}) collective-permute-start(bf16[512,512]{1,0:T(8,128)(2,1)S(1)} %get-tuple-element.16.x0), channel_id=1, source_target_pairs={{0,224},{32,0},{64,32},{96,64},{128,96},{160,128},{192,160},{224,1... | collective-permute-start | bytes 1572872 | tf_op jit(solution)/shard_map/ppermute | solution.py:305
  78.2 15.5 %collective-permute-start.4 = (bf16[512,512]{1,0:T(8,128)(2,1)S(1)}, bf16[512,512]{1,0:T(8,128)(2,1)S(1)}, u32[]{:S(2)}, u32[]{:S(2)}) collective-permute-start(bf16[512,512]{1,0:T(8,128)(2,1)S(1)} %get-tuple-element.16.x0), channel_id=1, source_target_pairs={{0,32},{32,64},{64,96},{96,128},{128,160},{160,192},{192,224},{224... | collective-permute-start | bytes 1572872 | tf_op jit(solution)/shard_map/ppermute | solution.py:304
  86.4 101.7 %copy-start.19 = (bf16[512,512]{1,0:T(8,128)(2,1)}, bf16[512,512]{1,0:T(8,128)(2,1)S(1)}, u32[]{:S(2)}) copy-start(bf16[512,512]{1,0:T(8,128)(2,1)S(1)} %collective-permute-done.8.b1) | copy-start | bytes 1572868
  86.4 28.0 %collective-permute-start.9 = (bf16[512,512]{1,0:T(8,128)(2,1)S(1)}, bf16[512,512]{1,0:T(8,128)(2,1)S(1)}, u32[]{:S(2)}, u32[]{:S(2)}) collective-permute-start(bf16[512,512]{1,0:T(8,128)(2,1)S(1)} %collective-permute-done.8.b1), channel_id=1, source_target_pairs={{0,224},{32,0},{64,32},{96,64},{128,96},{160,128},{192,160},{224,1... | collective-permute-start | bytes 1572872 | tf_op jit(solution)/shard_map/ppermute | solution.py:305
  91.2 68.4 %collective-permute-start.12 = (bf16[512,2048]{1,0:T(8,128)(2,1)}, bf16[512,2048]{1,0:T(8,128)(2,1)}, u32[]{:S(2)}, u32[]{:S(2)}) collective-permute-start(bf16[512,2048]{1,0:T(8,128)(2,1)} %bitcast.7.refs_0_), channel_id=1, source_target_pairs={{0,8},{8,0},{1,9},{9,1},{2,10},{10,2},{3,11},{11,3},{4,12},{12,4},... | collective-permute-start | bytes 6291464 | tf_op jit(solution)/shard_map/ppermute | solution.py:346
  92.6 95.4 %collective-permute-start.15 = (bf16[2048,512]{1,0:T(8,128)(2,1)}, bf16[2048,512]{1,0:T(8,128)(2,1)}, u32[]{:S(2)}, u32[]{:S(2)}) collective-permute-start(bf16[2048,512]{1,0:T(8,128)(2,1)} %bitcast.9.refs_4_), channel_id=1, source_target_pairs={{0,8},{8,0},{1,9},{9,1},{2,10},{10,2},{3,11},{11,3},{4,12},{12,4},... | collective-permute-start | bytes 6291464 | tf_op jit(solution)/shard_map/ppermute | solution.py:346
  92.6 95.4 %collective-permute-start.14 = (bf16[512,2048]{1,0:T(8,128)(2,1)}, bf16[512,2048]{1,0:T(8,128)(2,1)}, u32[]{:S(2)}, u32[]{:S(2)}) collective-permute-start(bf16[512,2048]{1,0:T(8,128)(2,1)} %all-gather.5.cloned.1.call-done.refs_2_), channel_id=1, source_target_pairs={{0,8},{8,0},{1,9},{9,1},{2,10},{10,2},{3,11},{11,3},{4,12},{12,4},... | collective-permute-start | bytes 6291464 | tf_op jit(solution)/shard_map/ppermute | solution.py:346
  114.4 73.7 %collective-permute-start.17 = (bf16[2048,512]{1,0:T(8,128)(2,1)}, bf16[2048,512]{1,0:T(8,128)(2,1)}, u32[]{:S(2)}, u32[]{:S(2)}) collective-permute-start(bf16[2048,512]{1,0:T(8,128)(2,1)} %all-gather.7.cloned.1.call-done.refs_6_), channel_id=1, source_target_pairs={{0,8},{8,0},{1,9},{9,1},{2,10},{10,2},{3,11},{11,3},{4,12},{12,4},... | collective-permute-start | bytes 6291464 | tf_op jit(solution)/shard_map/ppermute | solution.py:346
  114.4 15.9 %collective-permute-start.5 = (bf16[512,512]{1,0:T(8,128)(2,1)S(1)}, bf16[512,512]{1,0:T(8,128)(2,1)S(1)}, u32[]{:S(2)}, u32[]{:S(2)}) collective-permute-start(bf16[512,512]{1,0:T(8,128)(2,1)S(1)} %collective-permute-done.4.f1), channel_id=1, source_target_pairs={{0,32},{32,64},{64,96},{96,128},{128,160},{160,192},{192,224},{224... | collective-permute-start | bytes 1572872 | tf_op jit(solution)/shard_map/ppermute | solution.py:304
  130.3 29.3 %copy-start.22 = (bf16[512,512]{1,0:T(8,128)(2,1)}, bf16[512,512]{1,0:T(8,128)(2,1)S(1)}, u32[]{:S(2)}) copy-start(bf16[512,512]{1,0:T(8,128)(2,1)S(1)} %collective-permute-done.5.f2) | copy-start | bytes 1572868
  130.3 14.0 %collective-permute-start.10 = (bf16[512,512]{1,0:T(8,128)(2,1)S(1)}, bf16[512,512]{1,0:T(8,128)(2,1)S(1)}, u32[]{:S(2)}, u32[]{:S(2)}) collective-permute-start(bf16[512,512]{1,0:T(8,128)(2,1)S(1)} %collective-permute-done.9.b2), channel_id=1, source_target_pairs={{0,224},{32,0},{64,32},{96,64},{128,96},{160,128},{192,160},{224,1... | collective-permute-start | bytes 1572872 | tf_op jit(solution)/shard_map/ppermute | solution.py:305
  144.3 43.8 %copy-start.16 = (bf16[512,512]{1,0:T(8,128)(2,1)}, bf16[512,512]{1,0:T(8,128)(2,1)S(1)}, u32[]{:S(2)}) copy-start(bf16[512,512]{1,0:T(8,128)(2,1)S(1)} %collective-permute-done.10.b3) | copy-start | bytes 1572868
  144.3 14.0 %collective-permute-start.6 = (bf16[512,512]{1,0:T(8,128)(2,1)S(1)}, bf16[512,512]{1,0:T(8,128)(2,1)S(1)}, u32[]{:S(2)}, u32[]{:S(2)}) collective-permute-start(bf16[512,512]{1,0:T(8,128)(2,1)S(1)} %collective-permute-done.5.f2), channel_id=1, source_target_pairs={{0,32},{32,64},{64,96},{96,128},{128,160},{160,192},{192,224},{224... | collective-permute-start | bytes 1572872 | tf_op jit(solution)/shard_map/ppermute | solution.py:304
  158.3 29.8 %copy-start.17 = (bf16[512,512]{1,0:T(8,128)(2,1)}, bf16[512,512]{1,0:T(8,128)(2,1)S(1)}, u32[]{:S(2)}) copy-start(bf16[512,512]{1,0:T(8,128)(2,1)S(1)} %collective-permute-done.6.f3) | copy-start | bytes 1572868
  158.3 29.7 %collective-permute-start.11 = (bf16[256,512]{1,0:T(8,128)(2,1)S(1)}, bf16[256,512]{1,0:T(8,128)(2,1)S(1)}, u32[]{:S(2)}, u32[]{:S(2)}) collective-permute-start(bf16[256,512]{1,0:T(8,128)(2,1)S(1)} %slice.125), channel_id=1, source_target_pairs={{0,224},{32,0},{64,32},{96,64},{128,96},{160,128},{192,160},{224,1... | collective-permute-start | bytes 786440 | tf_op jit(solution)/shard_map/ppermute | solution.py:307
  159.6 28.4 %collective-permute-start.7 = (bf16[256,512]{1,0:T(8,128)(2,1)S(1)}, bf16[256,512]{1,0:T(8,128)(2,1)}, u32[]{:S(2)}, u32[]{:S(2)}) collective-permute-start(bf16[256,512]{1,0:T(8,128)(2,1)S(1)} %slice.124), channel_id=1, source_target_pairs={{0,32},{32,64},{64,96},{96,128},{128,160},{160,192},{192,224},{224... | collective-permute-start | bytes 786440 | tf_op jit(solution)/shard_map/ppermute | solution.py:306
  228.7 6.5 %collective-permute-start.18 = (bf16[256,512]{1,0:T(8,128)(2,1)S(1)}, bf16[256,512]{1,0:T(8,128)(2,1)S(1)}, u32[]{:S(2)}, u32[]{:S(2)}) collective-permute-start(bf16[256,512]{1,0:T(8,128)(2,1)S(1)} %get-tuple-element.29), channel_id=1, source_target_pairs={{0,224},{32,0},{64,32},{96,64},{128,96},{160,128},{192,160},{224,1... | collective-permute-start | bytes 786440 | tf_op jit(solution)/shard_map/ppermute | solution.py:319
  229.9 10.5 %collective-permute-start.28 = (bf16[256,512]{1,0:T(8,128)(2,1)S(1)}, bf16[256,512]{1,0:T(8,128)(2,1)S(1)}, u32[]{:S(2)}, u32[]{:S(2)}) collective-permute-start(bf16[256,512]{1,0:T(8,128)(2,1)S(1)} %get-tuple-element.30), channel_id=1, source_target_pairs={{0,32},{32,64},{64,96},{96,128},{128,160},{160,192},{192,224},{224... | collective-permute-start | bytes 786440 | tf_op jit(solution)/shard_map/ppermute | solution.py:320
  230.8 24.6 %copy-start.11 = (bf16[512,512]{1,0:T(8,128)(2,1)S(1)}, bf16[512,512]{1,0:T(8,128)(2,1)}, u32[]{:S(2)}) copy-start(bf16[512,512]{1,0:T(8,128)(2,1)} %get-tuple-element.23) | copy-start | bytes 1572868
  231.8 9.0 %collective-permute-start.25 = (bf16[256,512]{1,0:T(8,128)(2,1)S(1)}, bf16[256,512]{1,0:T(8,128)(2,1)S(1)}, u32[]{:S(2)}, u32[]{:S(2)}) collective-permute-start(bf16[256,512]{1,0:T(8,128)(2,1)S(1)} %slice.109), channel_id=1, source_target_pairs={{0,224},{32,0},{64,32},{96,64},{128,96},{160,128},{192,160},{224,1... | collective-permute-start | bytes 786440 | tf_op jit(solution)/shard_map/ppermute | solution.py:321
  236.2 10.3 %collective-permute-start.19 = (bf16[256,512]{1,0:T(8,128)(2,1)S(1)}, bf16[256,512]{1,0:T(8,128)(2,1)S(1)}, u32[]{:S(2)}, u32[]{:S(2)}) collective-permute-start(bf16[256,512]{1,0:T(8,128)(2,1)S(1)} %add_convert_fusion.9), channel_id=1, source_target_pairs={{0,224},{32,0},{64,32},{96,64},{128,96},{160,128},{192,160},{224,1... | collective-permute-start | bytes 786440 | tf_op jit(solution)/shard_map/ppermute | solution.py:324
  239.6 10.7 %collective-permute-start.22 = (bf16[256,512]{1,0:T(8,128)(2,1)S(1)}, bf16[256,512]{1,0:T(8,128)(2,1)S(1)}, u32[]{:S(2)}, u32[]{:S(2)}) collective-permute-start(bf16[256,512]{1,0:T(8,128)(2,1)S(1)} %slice.106), channel_id=1, source_target_pairs={{0,32},{32,64},{64,96},{96,128},{128,160},{160,192},{192,224},{224... | collective-permute-start | bytes 786440 | tf_op jit(solution)/shard_map/ppermute | solution.py:322
  240.4 15.1 %collective-permute-start.29 = (bf16[256,512]{1,0:T(8,128)(2,1)S(1)}, bf16[256,512]{1,0:T(8,128)(2,1)S(1)}, u32[]{:S(2)}, u32[]{:S(2)}) collective-permute-start(bf16[256,512]{1,0:T(8,128)(2,1)S(1)} %add_convert_fusion.2), channel_id=1, source_target_pairs={{0,32},{32,64},{64,96},{96,128},{128,160},{160,192},{192,224},{224... | collective-permute-start | bytes 786440 | tf_op jit(solution)/shard_map/ppermute | solution.py:325
  246.6 9.5 %collective-permute-start.20 = (bf16[256,512]{1,0:T(8,128)(2,1)S(1)}, bf16[256,512]{1,0:T(8,128)(2,1)S(1)}, u32[]{:S(2)}, u32[]{:S(2)}) collective-permute-start(bf16[256,512]{1,0:T(8,128)(2,1)S(1)} %get-tuple-element.27), channel_id=1, source_target_pairs={{0,224},{32,0},{64,32},{96,64},{128,96},{160,128},{192,160},{224,1... | collective-permute-start | bytes 786440 | tf_op jit(solution)/shard_map/ppermute | solution.py:324
  250.2 8.7 %collective-permute-start.26 = (bf16[256,512]{1,0:T(8,128)(2,1)S(1)}, bf16[256,512]{1,0:T(8,128)(2,1)S(1)}, u32[]{:S(2)}, u32[]{:S(2)}) collective-permute-start(bf16[256,512]{1,0:T(8,128)(2,1)S(1)} %get-tuple-element.28), channel_id=1, source_target_pairs={{0,224},{32,0},{64,32},{96,64},{128,96},{160,128},{192,160},{224,1... | collective-permute-start | bytes 786440 | tf_op jit(solution)/shard_map/ppermute | solution.py:327
  255.6 10.4 %collective-permute-start.23 = (bf16[256,512]{1,0:T(8,128)(2,1)S(1)}, bf16[256,512]{1,0:T(8,128)(2,1)S(1)}, u32[]{:S(2)}, u32[]{:S(2)}) collective-permute-start(bf16[256,512]{1,0:T(8,128)(2,1)S(1)} %get-tuple-element.33), channel_id=1, source_target_pairs={{0,32},{32,64},{64,96},{96,128},{128,160},{160,192},{192,224},{224... | collective-permute-start | bytes 786440 | tf_op jit(solution)/shard_map/ppermute | solution.py:328
  255.7 15.3 %collective-permute-start.30 = (bf16[256,512]{1,0:T(8,128)(2,1)S(1)}, bf16[256,512]{1,0:T(8,128)(2,1)S(1)}, u32[]{:S(2)}, u32[]{:S(2)}) collective-permute-start(bf16[256,512]{1,0:T(8,128)(2,1)S(1)} %get-tuple-element.34), channel_id=1, source_target_pairs={{0,32},{32,64},{64,96},{96,128},{128,160},{160,192},{192,224},{224... | collective-permute-start | bytes 786440 | tf_op jit(solution)/shard_map/ppermute | solution.py:325
  259.0 15.4 %collective-permute-start.21 = (bf16[256,512]{1,0:T(8,128)(2,1)S(1)}, bf16[256,512]{1,0:T(8,128)(2,1)S(1)}, u32[]{:S(2)}, u32[]{:S(2)}) collective-permute-start(bf16[256,512]{1,0:T(8,128)(2,1)S(1)} %get-tuple-element.25), channel_id=1, source_target_pairs={{0,224},{32,0},{64,32},{96,64},{128,96},{160,128},{192,160},{224,1... | collective-permute-start | bytes 786440 | tf_op jit(solution)/shard_map/ppermute | solution.py:324
  271.1 7.7 %collective-permute-start.24 = (bf16[256,512]{1,0:T(8,128)(2,1)S(1)}, bf16[256,512]{1,0:T(8,128)(2,1)S(1)}, u32[]{:S(2)}, u32[]{:S(2)}) collective-permute-start(bf16[256,512]{1,0:T(8,128)(2,1)S(1)} %get-tuple-element.31), channel_id=1, source_target_pairs={{0,32},{32,64},{64,96},{96,128},{128,160},{160,192},{192,224},{224... | collective-permute-start | bytes 786440 | tf_op jit(solution)/shard_map/ppermute | solution.py:328
  271.2 7.6 %collective-permute-start.27 = (bf16[256,512]{1,0:T(8,128)(2,1)S(1)}, bf16[256,512]{1,0:T(8,128)(2,1)S(1)}, u32[]{:S(2)}, u32[]{:S(2)}) collective-permute-start(bf16[256,512]{1,0:T(8,128)(2,1)S(1)} %get-tuple-element.26), channel_id=1, source_target_pairs={{0,224},{32,0},{64,32},{96,64},{128,96},{160,128},{192,160},{224,1... | collective-permute-start | bytes 786440 | tf_op jit(solution)/shard_map/ppermute | solution.py:327
  274.4 7.6 %collective-permute-start.31 = (bf16[256,512]{1,0:T(8,128)(2,1)S(1)}, bf16[256,512]{1,0:T(8,128)(2,1)S(1)}, u32[]{:S(2)}, u32[]{:S(2)}) collective-permute-start(bf16[256,512]{1,0:T(8,128)(2,1)S(1)} %get-tuple-element.32), channel_id=1, source_target_pairs={{0,32},{32,64},{64,96},{96,128},{128,160},{160,192},{192,224},{224... | collective-permute-start | bytes 786440 | tf_op jit(solution)/shard_map/ppermute | solution.py:325
  (10 other events, 140.3 us)
Sparse Core Ops, SparseCore 0:
  16.5 49.4 all-gather.4
  67.8 46.4 all-gather.6
